TPU v7x, 32 devices: a whole 2x2x4 slice. The times are simulated.
32 devices in a mesh: rve: 4 (over z), gy: 2 (over x), gz: 4 (over y, core).
Axes of the slice: x: 2, y: 2, z: 4, core: 2. Of those that a mesh axis runs over, the one named last changes fastest.
Arguments:
- strain: float32 [32, 6], P('rve'), may hold values from -6 to 6
- tangent: float32 [32], P('rve'), may hold values from 0.5 to 2
- yield_list: int32 [16], P('rve'), may hold values from 0 to 7, as said below
- destination: int32 [16, 1], P('rve'), may hold values from 0 to 3; in each aligned block of 4 rows (0 to 3, 4 to 7, ...) at most 2 rows name the same one
- phase_map: int32 [4, 8, 32, 128], P('rve', 'gy', 'gz'), may hold values from 0 to 1
- polarization: float32 [4, 3, 6, 8, 32, 128], P('rve', None, None, 'gy', 'gz'), may hold values from -6 to 6
- stencil: float32 [3, 3, 27], replicated, may hold values from -0.6 to 3, as said below
Outputs:
- fields: float32 [4, 8, 3, 8, 32, 128], P('rve', None, None, 'gy', 'gz')
- stress_rows: float32 [16, 6], P('rve')
Inputs may be any that keep to these rules, and one draw needn't show every extreme that they name: `yield_list`: the 4 entries of each macro device are distinct local point numbers, and each device lists 0 and 7. `destination`: among the 4 entries of one macro device, no group is named more than 2 times. stencil[c, d, o] equals stencil[d, c, 26 - o] for all channels and offsets.
All inputs are finite; a program needn't handle non-finite values.
Results may differ from a plain program's by a relative error of at most 0.0003.
Values sent between devices are 32-bit elements; how exact they have to be, the bound alone decides.
A program may use at most 192 MiB of HBM per device.

v0:
```python
import jax
import jax.numpy as jnp
from jax import lax
from jax.sharding import PartitionSpec as P

CAP = 2
SWEEPS = 6


FULL_PRECISION = lax.Precision.HIGHEST
LOWER_BOUND = 0.05
UPPER_BOUND = 1.95


def padded(block, sides, width):
    for axis, dim in sides:
        count = lax.axis_size(axis)
        forward = [(i, i + 1) for i in range(count - 1)]
        forward.append((count - 1, 0))
        backward = [(target, source) for source, target in forward]
        low = lax.ppermute(
            lax.slice_in_dim(block, block.shape[dim] - width, None, axis=dim), axis, forward
        )
        high = lax.ppermute(lax.slice_in_dim(block, 0, width, axis=dim), axis, backward)
        block = jnp.concatenate([low, block, high], axis=dim)
    return block


def chebyshev_weights(sweep_count):
    centre_value = 0.5 * (UPPER_BOUND + LOWER_BOUND)
    half_width = 0.5 * (UPPER_BOUND - LOWER_BOUND)
    ratio_value = centre_value / half_width
    rho_before = 1.0 / ratio_value
    weights = []
    for sweep_index in range(1, sweep_count):
        rho_after = 1.0 / (2.0 * ratio_value - rho_before)
        weights.append((rho_after * rho_before, 2.0 * rho_after / half_width))
        rho_before = rho_after
    return (1.0 / centre_value, weights)


def trim_margin(values_in, margin_have, margin_want, first_dim):
    excess = margin_have - margin_want
    values_in = lax.slice_in_dim(
        values_in, excess, values_in.shape[first_dim] - excess, axis=first_dim
    )
    return lax.slice_in_dim(
        values_in, excess, values_in.shape[first_dim + 1] - excess, axis=first_dim + 1
    )


def apply_stiffness(field_now, moduli, stencil):
    inner_y = field_now.shape[2] - 2
    inner_z = field_now.shape[3] - 2
    centre_mod = moduli[:, 1 : 1 + inner_y, 1 : 1 + inner_z, :]
    running = [None, None, None]
    for shift_y in (-1, 0, 1):
        for shift_z in (-1, 0, 1):
            shifted = field_now[
                :, :, 1 + shift_y : 1 + shift_y + inner_y, 1 + shift_z : 1 + shift_z + inner_z, :
            ]
            shifted_mod = moduli[
                :, 1 + shift_y : 1 + shift_y + inner_y, 1 + shift_z : 1 + shift_z + inner_z, :
            ]
            for shift_x in (-1, 0, 1):
                if shift_x != 0:
                    rolled = jnp.roll(shifted, -shift_x, axis=4)
                    rolled_mod = jnp.roll(shifted_mod, -shift_x, axis=3)
                else:
                    rolled = shifted
                    rolled_mod = shifted_mod
                offset_index = (shift_y + 1) * 9 + (shift_z + 1) * 3 + (shift_x + 1)
                edge_mod = 0.5 * (centre_mod + rolled_mod)
                weighted = [edge_mod * rolled[:, channel_in] for channel_in in range(3)]
                for channel_out in range(3):
                    mixed = stencil[channel_out, 0, offset_index] * weighted[0]
                    mixed = mixed + stencil[channel_out, 1, offset_index] * weighted[1]
                    mixed = mixed + stencil[channel_out, 2, offset_index] * weighted[2]
                    if running[channel_out] is None:
                        running[channel_out] = mixed
                    else:
                        running[channel_out] = running[channel_out] + mixed
    return jnp.stack(running, axis=1)


def body(strain, tangent, yield_list, destination, phase_map, polarization, stencil):
    groups = lax.axis_size("rve")
    rows_here = strain.shape[0]
    yield_count = yield_list.shape[0]
    picker = (jnp.arange(rows_here, dtype=jnp.int32)[None, :] == yield_list[:, None]).astype(
        jnp.float32
    )
    row_strain = jnp.dot(picker, strain, precision=FULL_PRECISION)
    row_tangent = jnp.dot(picker, tangent, precision=FULL_PRECISION)
    target = destination[:, 0]
    positions = jnp.arange(yield_count, dtype=jnp.int32)
    earlier = (target[:, None] == target[None, :]) & (positions[None, :] < positions[:, None])
    rank_in = jnp.sum(earlier.astype(jnp.int32), axis=1)
    group_ids = jnp.arange(groups, dtype=jnp.int32)
    slot_ids = jnp.arange(CAP, dtype=jnp.int32)
    onehot = (
        (target[None, None, :] == group_ids[:, None, None])
        & (rank_in[None, None, :] == slot_ids[None, :, None])
    ).astype(jnp.float32)
    packet = jnp.einsum("gci,ij->gcj", onehot, row_strain, precision=FULL_PRECISION)
    packet_tangent = (
        jnp.einsum("gci,i->gc", onehot, row_tangent, precision=FULL_PRECISION)
        + 1.0
        - jnp.sum(onehot, axis=2)
    )
    parcel = jnp.concatenate([packet, packet_tangent[:, :, None]], axis=2)
    arrived = lax.all_to_all(parcel, "rve", split_axis=0, concat_axis=0, tiled=True)
    slot_strain = arrived[:, :, :6].reshape(groups * CAP, 6)
    slot_tangent = arrived[:, :, 6].reshape(groups * CAP)
    phase_wide = padded(phase_map[0], (("gy", 0), ("gz", 1)), 2)
    moduli_wide = jnp.where(
        phase_wide[None] == 1, slot_tangent[:, None, None, None], jnp.float32(1.0)
    )
    moduli_core = trim_margin(moduli_wide, 2, 0, 1)
    moduli_one = trim_margin(moduli_wide, 2, 1, 1)
    polar_local = polarization[0]
    centre_diag = jnp.diagonal(stencil[:, :, 13])
    body_force = moduli_core[:, None] * jnp.einsum(
        "cjyzx,lj->lcyzx", polar_local, slot_strain, precision=FULL_PRECISION
    )
    inverse_diag = 1.0 / (centre_diag[None, :, None, None, None] * moduli_core[:, None])
    first_weight, weights = chebyshev_weights(SWEEPS)
    update = first_weight * (body_force * inverse_diag)
    field_now = update
    for old_weight, new_weight in weights:
        wrapped = padded(field_now, (("gy", 2), ("gz", 3)), 1)
        residual_now = body_force - apply_stiffness(wrapped, moduli_one, stencil)
        update = old_weight * update + new_weight * (residual_now * inverse_diag)
        field_now = field_now + update
    coupled = jnp.einsum(
        "cjyzx,lcyzx->lj", polar_local, moduli_core[:, None] * field_now, precision=FULL_PRECISION
    )
    partial_value = coupled + slot_strain * jnp.sum(moduli_core, axis=(1, 2, 3))[:, None]
    total_cells = (
        lax.axis_size("gy")
        * lax.axis_size("gz")
        * field_now.shape[2]
        * field_now.shape[3]
        * field_now.shape[4]
    )
    summed = lax.psum(partial_value, ("gy", "gz")) / total_cells
    returned = lax.all_to_all(
        summed.reshape(groups, CAP, 6), "rve", split_axis=0, concat_axis=0, tiled=True
    )
    stress_rows = jnp.einsum("gci,gcj->ij", onehot, returned, precision=FULL_PRECISION)
    return (field_now[None], stress_rows)


def solution(mesh):
    return jax.shard_map(
        body,
        mesh=mesh,
        in_specs=(
            P("rve", None),
            P("rve"),
            P("rve"),
            P("rve", None),
            P("rve", "gy", "gz", None),
            P("rve", None, None, "gy", "gz", None),
            P(),
        ),
        out_specs=(P("rve", None, None, "gy", "gz", None), P("rve", None)),
        check_vma=False,
    )
```

profile of v0, /device:TPU:0, one launch (start us, length us, event | category | flops | bytes accessed | tf_op | source)
XLA Modules:
  0.0 913.6 jit_solution(3795321326773116138)
XLA Ops:
  4.4 6.3 all-to-all-start
  10.7 1.6 collective-permute-start.1
  13.0 0.7 fusion.1290
  13.7 0.7 fusion.1298
  15.2 0.7 fusion.1300
  16.6 0.7 fusion.1291
  17.3 0.7 fusion.1292
  18.0 0.7 fusion.1293
  18.8 0.7 fusion.1294
  19.5 0.7 fusion.1295
  20.2 0.7 fusion.1296
  21.7 0.7 fusion.1289
  23.9 0.7 collective-permute-done.3
  24.6 1.8 collective-permute-done.2
  27.6 1.6 collective-permute-start.5
  29.7 1.4 fusion.1285
  31.1 2.2 collective-permute-done.5
  33.3 1.2 collective-permute-done.4
  34.6 2.0 collective-permute-start.7
  38.7 0.9 fusion.1276
  39.6 0.9 fusion.1277
  41.2 56.3 %add_bitcast_fusion.14 = (f32[8,1,4,8,128]{4,0,3,2,1:T(8,128)S(1)}, f32[8,4,8,128]{3,0,2,1:T(8,128)S(1)}, f32[8,4,8,128]{3,0,2,1:T(8,128)S(1)}, f32[8,4,8,128]{3...) fusion(f32[8,4,8,128]{3,0,2,1:T(8,128)S(1)} %get-tuple-element., ...), kind=kLoop, calls=%fused_computation.1681 | loop fusion | flops 11108352 | bytes 28126532 | tf_op jit(solution)/shard_map/stack | solution.py:83
  97.5 52.1 %add_bitcast_fusion.12 = f32[8,1,4,8,128]{4,0,3,2,1:T(8,128)S(1)} fusion(f32[8,4,8,128]{3,0,2,1:T(8,128)S(1)} %get-tuple-element.309, f32[8,4,8,128]{3,0,2,1:T(8,128)S(1)} %get-tuple-element.308, f32[8,4,8,128]{3,0,2,1:T(8,128)S(1)} %get-tuple-element.474, f32[8,4,8,128]{3,0,2,1:T(8,128)S(1)} %get-tuple-element.307, ...), kind=kLoop, calls=%fused_computation.1679 | loop fusion | flops 6225920 | bytes 11927876 | tf_op jit(solution)/shard_map/stack | solution.py:83
  149.5 51.4 %add_bitcast_fusion.13 = f32[8,1,4,8,128]{4,0,3,2,1:T(8,128)S(1)} fusion(f32[8,4,8,128]{3,0,2,1:T(8,128)S(1)} %get-tuple-element.309, f32[8,4,8,128]{3,0,2,1:T(8,128)S(1)} %get-tuple-element.308, f32[8,4,8,128]{3,0,2,1:T(8,128)S(1)} %get-tuple-element.474, f32[8,4,8,128]{3,0,2,1:T(8,128)S(1)} %get-tuple-element.307, ...), kind=kLoop, calls=%fused_computation.1680 | loop fusion | flops 6225920 | bytes 11927876 | tf_op jit(solution)/shard_map/stack | solution.py:83
  201.2 1.6 collective-permute-start.9
  203.3 3.6 collective-permute-done.9
  207.0 2.0 collective-permute-done.8
  209.2 0.8 collective-permute-start.10
  211.2 2.5 collective-permute-done.10
  215.5 54.6 %add_bitcast_fusion.11 = (f32[8,1,4,8,128]{4,0,3,2,1:T(8,128)S(1)}, f32[8,4,8,128]{3,0,2,1:T(8,128)S(1)}, f32[8,4,8,128]{3,0,2,1:T(8,128)S(1)}, f32[8,4,8,128]{3...) fusion(f32[]{:T(128)} %bitcast.175, ...), kind=kLoop, calls=%fused_computation.1678 | loop fusion | flops 9764864 | bytes 27459908 | tf_op jit(solution)/shard_map/stack | solution.py:83
  270.1 52.2 %add_bitcast_fusion.9 = f32[8,1,4,8,128]{4,0,3,2,1:T(8,128)S(1)} fusion(f32[8,4,8,128]{3,0,2,1:T(8,128)S(1)} %get-tuple-element.229, f32[8,4,8,128]{3,0,2,1:T(8,128)S(1)} %get-tuple-element.228, f32[8,4,8,128]{3,0,2,1:T(8,128)S(1)} %get-tuple-element.227, f32[8,4,8,128]{3,0,2,1:T(8,128)S(1)} %get-tuple-element.226, ...), kind=kLoop, calls=%fused_computation.1676 | loop fusion | flops 6225920 | bytes 11927876 | tf_op jit(solution)/shard_map/stack | solution.py:83
  322.4 51.6 %add_bitcast_fusion.10 = f32[8,1,4,8,128]{4,0,3,2,1:T(8,128)S(1)} fusion(f32[8,4,8,128]{3,0,2,1:T(8,128)S(1)} %get-tuple-element.229, f32[8,4,8,128]{3,0,2,1:T(8,128)S(1)} %get-tuple-element.228, f32[8,4,8,128]{3,0,2,1:T(8,128)S(1)} %get-tuple-element.227, f32[8,4,8,128]{3,0,2,1:T(8,128)S(1)} %get-tuple-element.226, ...), kind=kLoop, calls=%fused_computation.1677 | loop fusion | flops 6225920 | bytes 11927876 | tf_op jit(solution)/shard_map/stack | solution.py:83
  374.3 1.0 collective-permute-start.13
  375.3 1.1 collective-permute-start.12
  376.4 3.3 collective-permute-done.13
  379.7 1.1 collective-permute-done.12
  382.6 0.8 collective-permute-done.15
  383.4 1.4 collective-permute-done.14
  386.6 54.6 %add_bitcast_fusion.8 = (f32[8,1,4,8,128]{4,0,3,2,1:T(8,128)S(1)}, f32[8,4,8,128]{3,0,2,1:T(8,128)S(1)}, f32[8,4,8,128]{3,0,2,1:T(8,128)S(1)}, f32[8,4,8,128]{3,...) fusion(f32[]{:T(128)} %bitcast.175, ...), kind=kLoop, calls=%fused_computation.1675 | loop fusion | flops 9764864 | bytes 27459908 | tf_op jit(solution)/shard_map/stack | solution.py:83
  441.3 52.2 %add_bitcast_fusion.6 = f32[8,1,4,8,128]{4,0,3,2,1:T(8,128)S(1)} fusion(f32[8,4,8,128]{3,0,2,1:T(8,128)S(1)} %get-tuple-element.174, f32[8,4,8,128]{3,0,2,1:T(8,128)S(1)} %get-tuple-element.173, f32[8,4,8,128]{3,0,2,1:T(8,128)S(1)} %get-tuple-element.172, f32[8,4,8,128]{3,0,2,1:T(8,128)S(1)} %get-tuple-element.171, ...), kind=kLoop, calls=%fused_computation.1673 | loop fusion | flops 6225920 | bytes 11927876 | tf_op jit(solution)/shard_map/stack | solution.py:83
  493.5 51.6 %add_bitcast_fusion.7 = f32[8,1,4,8,128]{4,0,3,2,1:T(8,128)S(1)} fusion(f32[8,4,8,128]{3,0,2,1:T(8,128)S(1)} %get-tuple-element.174, f32[8,4,8,128]{3,0,2,1:T(8,128)S(1)} %get-tuple-element.173, f32[8,4,8,128]{3,0,2,1:T(8,128)S(1)} %get-tuple-element.172, f32[8,4,8,128]{3,0,2,1:T(8,128)S(1)} %get-tuple-element.171, ...), kind=kLoop, calls=%fused_computation.1674 | loop fusion | flops 6225920 | bytes 11927876 | tf_op jit(solution)/shard_map/stack | solution.py:83
  545.5 0.8 collective-permute-start.17
  546.3 1.3 collective-permute-start.16
  547.6 2.6 collective-permute-done.17
  550.2 1.1 collective-permute-done.16
  551.2 1.1 collective-permute-start.19
  554.3 2.4 collective-permute-done.18
  558.5 54.5 %add_bitcast_fusion.5 = (f32[8,1,4,8,128]{4,0,3,2,1:T(8,128)S(1)}, f32[8,4,8,128]{3,0,2,1:T(8,128)S(1)}, f32[8,4,8,128]{3,0,2,1:T(8,128)S(1)}, f32[8,4,8,128]{3,...) fusion(f32[]{:T(128)} %bitcast.175, ...), kind=kLoop, calls=%fused_computation.1672 | loop fusion | flops 9764864 | bytes 27459908 | tf_op jit(solution)/shard_map/stack | solution.py:83
  613.0 52.1 %add_bitcast_fusion.3 = f32[8,1,4,8,128]{4,0,3,2,1:T(8,128)S(1)} fusion(f32[8,4,8,128]{3,0,2,1:T(8,128)S(1)} %get-tuple-element.117, f32[8,4,8,128]{3,0,2,1:T(8,128)S(1)} %get-tuple-element.116, f32[8,4,8,128]{3,0,2,1:T(8,128)S(1)} %get-tuple-element.115, f32[8,4,8,128]{3,0,2,1:T(8,128)S(1)} %get-tuple-element.114, ...), kind=kLoop, calls=%fused_computation.1670 | loop fusion | flops 6225920 | bytes 11927876 | tf_op jit(solution)/shard_map/stack | solution.py:83
  665.1 51.5 %add_bitcast_fusion.4 = f32[8,1,4,8,128]{4,0,3,2,1:T(8,128)S(1)} fusion(f32[8,4,8,128]{3,0,2,1:T(8,128)S(1)} %get-tuple-element.117, f32[8,4,8,128]{3,0,2,1:T(8,128)S(1)} %get-tuple-element.116, f32[8,4,8,128]{3,0,2,1:T(8,128)S(1)} %get-tuple-element.115, f32[8,4,8,128]{3,0,2,1:T(8,128)S(1)} %get-tuple-element.114, ...), kind=kLoop, calls=%fused_computation.1671 | loop fusion | flops 6225920 | bytes 11927876 | tf_op jit(solution)/shard_map/stack | solution.py:83
  717.5 1.4 collective-permute-start.20
  718.9 3.5 collective-permute-done.21
  722.4 1.1 collective-permute-done.20
  723.5 0.7 collective-permute-start.22
  726.0 1.6 collective-permute-done.22
  729.4 54.5 %add_bitcast_fusion.2 = (f32[8,1,4,8,128]{4,0,3,2,1:T(8,128)S(1)}, f32[8,4,8,128]{3,0,2,1:T(8,128)S(1)}, f32[8,4,8,128]{3,0,2,1:T(8,128)S(1)}, f32[8,4,8,128]{3,...) fusion(f32[]{:T(128)} %bitcast.175, ...), kind=kLoop, calls=%fused_computation.1669 | loop fusion | flops 9764864 | bytes 27459908 | tf_op jit(solution)/shard_map/stack | solution.py:83
  784.0 52.1 %add_bitcast_fusion = f32[8,1,4,8,128]{4,0,3,2,1:T(8,128)S(1)} fusion(f32[8,4,8,128]{3,0,2,1:T(8,128)S(1)} %get-tuple-element.62, f32[8,4,8,128]{3,0,2,1:T(8,128)S(1)} %get-tuple-element.61, f32[8,4,8,128]{3,0,2,1:T(8,128)S(1)} %get-tuple-element.60, f32[8,4,8,128]{3,0,2,1:T(8,128)S(1)} %get-tuple-element.59, f32[8,4,8,128]{3,0,2,1:T(8,128)S(1)} %get-tuple-element.58, ...), kind=kLoop, calls=%fused_computation.1667 | loop fusion | flops 6225920 | bytes 11927876 | tf_op jit(solution)/shard_map/stack | solution.py:83
  836.1 51.5 %add_bitcast_fusion.1 = f32[8,1,4,8,128]{4,0,3,2,1:T(8,128)S(1)} fusion(f32[8,4,8,128]{3,0,2,1:T(8,128)S(1)} %get-tuple-element.62, f32[8,4,8,128]{3,0,2,1:T(8,128)S(1)} %get-tuple-element.61, f32[8,4,8,128]{3,0,2,1:T(8,128)S(1)} %get-tuple-element.60, f32[8,4,8,128]{3,0,2,1:T(8,128)S(1)} %get-tuple-element.59, f32[8,4,8,128]{3,0,2,1:T(8,128)S(1)} %get-tuple-element.58, ...), kind=kLoop, calls=%fused_computation.1668 | loop fusion | flops 6225920 | bytes 11927876 | tf_op jit(solution)/shard_map/stack | solution.py:83
  887.8 1.0 fusion
  888.9 12.4 %psum.7 = f32[8,6]{1,0:T(8,128)S(1)} all-reduce(f32[8,6]{1,0:T(8,128)S(1)} %fusion), channel_id=1, replica_groups=mesh['rve'=4,'gy'=2,'gz'=4] {'gy','gz'}, use_global_device_ids=true, to_apply=%region_3.4 | all-reduce | flops 48 | bytes 384 | tf_op jit(solution)/shard_map/psum | solution.py:146
  901.9 5.0 all-to-all-start.1
  906.9 0.8 copy.31
  907.7 4.8 all-to-all-done.1
  912.5 0.8 convolution_bitcast_fusion.2
  (117 shorter events, 30.0 us)
Async XLA Ops:
  0.6 26.3 %copy-start = (f32[1,3,6,4,8,128]{5,4,3,2,1,0:T(8,128)S(1)}, f32[1,3,6,4,8,128]{5,4,3,2,1,0:T(8,128)}, u32[]{:S(2)}) copy-start(f32[1,3,6,4,8,128]{5,4,3,2,1,0:T(8,128)} %param.12) | copy-start | bytes 884740
  0.6 0.7 copy-start.4
  1.5 0.7 copy-start.5
  1.5 0.7 copy-start.6
  2.6 0.7 copy-start.3
  3.7 7.0 copy-start.2
  4.4 19.3 %all-to-all-start = ((f32[4,2,7]{2,1,0:T(2,128)}), f32[4,2,7]{2,1,0:T(2,128)S(1)}, u32[]{:S(2)}, u32[]{:S(2)}) async-start(f32[4,2,7]{2,1,0:T(2,128)} %copy.27), calls=%async_computation | async-start | bytes 8192 | tf_op jit(solution)/shard_map/all_to_all | solution.py:112
  10.7 2.1 copy-start.1
  10.7 12.3 %collective-permute-start.1 = (s32[2,8,128]{2,1,0:T(8,128)S(1)}, s32[2,8,128]{2,1,0:T(8,128)S(1)}, u32[]{:S(2)}, u32[]{:S(2)}) collective-permute-start(s32[2,8,128]{2,1,0:T(8,128)S(1)} %get-tuple-element.577), channel_id=1, source_target_pairs={{4,0},{0,4},{5,1},{1,5},{6,2},{2,6},{7,3},{3,7},{12,8},{8,12},{13,... | collective-permute-start | bytes 24584 | tf_op jit(solution)/shard_map/ppermute | solution.py:24
  12.3 10.8 %collective-permute-start = (s32[2,8,128]{2,1,0:T(8,128)S(1)}, s32[2,8,128]{2,1,0:T(8,128)S(1)}, u32[]{:S(2)}, u32[]{:S(2)}) collective-permute-start(s32[2,8,128]{2,1,0:T(8,128)S(1)} %get-tuple-element.576), channel_id=1, source_target_pairs={{0,4},{4,0},{1,5},{5,1},{2,6},{6,2},{3,7},{7,3},{8,12},{12,8},{9,1... | collective-permute-start | bytes 24584 | tf_op jit(solution)/shard_map/ppermute | solution.py:21
  23.1 1.5 collective-permute-start.3
  23.3 3.1 collective-permute-start.2
  27.6 5.7 collective-permute-start.5
  29.2 5.4 collective-permute-start.4
  34.6 3.8 collective-permute-start.6
  34.6 4.0 collective-permute-start.7
  201.2 5.7 collective-permute-start.9
  202.8 6.1 collective-permute-start.8
  209.0 2.3 collective-permute-start.11
  209.2 4.5 collective-permute-start.10
  374.3 5.4 collective-permute-start.13
  375.3 5.5 collective-permute-start.12
  380.8 2.6 collective-permute-start.15
  380.8 4.0 collective-permute-start.14
  545.5 4.7 collective-permute-start.17
  546.3 5.0 collective-permute-start.16
  551.2 3.1 collective-permute-start.19
  552.3 4.3 collective-permute-start.18
  716.8 5.6 collective-permute-start.21
  717.5 6.0 collective-permute-start.20
  723.5 2.5 collective-permute-start.23
  723.5 4.1 collective-permute-start.22
  901.9 10.6 %all-to-all-start.1 = ((f32[4,2,6]{2,1,0:T(2,128)}), f32[4,2,6]{2,1,0:T(2,128)S(1)}, u32[]{:S(2)}, u32[]{:S(2)}) async-start(f32[4,2,6]{2,1,0:T(2,128)} %bitcast.681), calls=%async_computation.1 | async-start | bytes 8192 | tf_op jit(solution)/shard_map/all_to_all | solution.py:147
where the time goes:
time: 928 us; the launch traced here: 914 us
  other arithmetic  802 us (86%)
  waiting for transfers between devices  39.9 us (4%)
  starting transfers between devices  30.4 us (3%)
  local copies, waits for them, and re-layouts  24.1 us (3%)
  blocking collectives  12.4 us (1%)
    another operation x15, other arithmetic, apply_stiffness(): return jnp.stack(running, axis=1)  793 us
  transfers between devices with their start and end apart: 26, of which 23 were waited for; matrix products, arithmetic and copies ran while one was open for 2% of the time, Pallas kernels for 0%

commit v1 on v0

--- a/solution.py
+++ b/solution.py
@@ -1,10 +1,16 @@
+import functools
+
 import jax
 import jax.numpy as jnp
 from jax import lax
+from jax.experimental import pallas as pl
+from jax.experimental.pallas import tpu as pltpu
 from jax.sharding import PartitionSpec as P
 
 CAP = 2
 SWEEPS = 6
+MESH = pl.DeviceIdType.MESH
+TANGENT, TARGET, RANK, LISTED = 6, 7, 8, 9
 
 
 FULL_PRECISION = lax.Precision.HIGHEST
@@ -151,9 +157,397 @@
     return (field_now[None], stress_rows)
 
 
+def kernel(
+    groups, ngy, ngz,
+    strain, tangent, yield_list, destination, stencil, phase, polar,
+    fields, rows_out,
+    tables, slots, phase_all, force_out, force, matrix, spread, field_now, update,
+    mod_mid, mod_low, mod_high, mod_inv, sums, partials, totals,
+    table_send, table_recv, phase_send, phase_recv, force_send, force_recv,
+    field_send, field_recv, part_send, part_recv, total_send, total_recv,
+):
+    f32, bf16 = jnp.float32, jnp.bfloat16
+    channels, strains = polar.shape[1], polar.shape[2]
+    y_here, z_here, nx = polar.shape[3:]
+    ny, nz = y_here * ngy, z_here * ngz
+    wide = channels * nz
+    slot_rows = 3 * wide
+    depth = 3 * slot_rows
+    listed = yield_list.shape[0]
+    loads = groups * CAP
+    my_r, my_y, my_z = lax.axis_index("rve"), lax.axis_index("gy"), lax.axis_index("gz")
+    my_load = my_y * ngz + my_z
+
+    def turned(base, step, count):
+        return lax.rem(base + step + count, count)
+
+    mates = [(dy, dz) for dy in list(range(1, ngy)) + [0] for dz in list(range(1, ngz)) + [0]]
+    others = [mate for mate in mates if mate != (0, 0)]
+
+    def mate_id(dy, dz):
+        return {"gy": turned(my_y, dy, ngy), "gz": turned(my_z, dz, ngz)}
+
+    def block(dy, dz):
+        y_at = turned(my_y, dy, ngy) * y_here
+        z_at = pl.multiple_of(turned(my_z, dz, ngz) * z_here, 8)
+        return pl.ds(y_at, y_here), pl.ds(z_at, z_here)
+
+    barrier = pltpu.get_barrier_semaphore()
+    for dy, dz in others:
+        pl.semaphore_signal(barrier, inc=1, device_id=mate_id(dy, dz), device_id_type=MESH)
+    for step in range(1, groups):
+        pl.semaphore_signal(
+            barrier, inc=1, device_id={"rve": turned(my_r, step, groups)}, device_id_type=MESH
+        )
+
+    row_ids = lax.broadcasted_iota(jnp.int32, (8, 128), 0)
+    lane_ids = lax.broadcasted_iota(jnp.int32, (8, 128), 1)
+    table = jnp.zeros((8, 128), f32)
+    for i in range(listed):
+        point, target = yield_list[i], destination[i, 0]
+        rank = jnp.int32(0)
+        for k in range(i):
+            rank = rank + jnp.where(destination[k, 0] == target, 1, 0)
+        values = [strain[point, j] for j in range(strains)]
+        values += [tangent[point], target.astype(f32), rank.astype(f32), jnp.float32(1.0)]
+        for j, value in enumerate(values):
+            table = jnp.where((row_ids == i) & (lane_ids == j), value, table)
+    tables[my_r] = table
+
+    pl.semaphore_wait(barrier, len(others) + groups - 1)
+
+    def table_copy(step, owner):
+        return pltpu.make_async_remote_copy(
+            src_ref=tables.at[my_r], dst_ref=tables.at[owner],
+            send_sem=table_send.at[step], recv_sem=table_recv.at[step],
+            device_id={"rve": turned(my_r, step, groups)}, device_id_type=MESH,
+        )
+
+    def phase_copy(index, dy, dz):
+        y_at, z_at = block(dy, dz)
+        to_y, to_z = others[index]
+        return pltpu.make_async_remote_copy(
+            src_ref=phase.at[0], dst_ref=phase_all.at[y_at, z_at],
+            send_sem=phase_send.at[index], recv_sem=phase_recv.at[index],
+            device_id=mate_id(to_y, to_z), device_id_type=MESH,
+        )
+
+    for step in range(1, groups):
+        table_copy(step, my_r).start()
+    for index in range(len(others)):
+        phase_copy(index, 0, 0).start()
+    own_y, own_z = block(0, 0)
+    phase_all[own_y, own_z, :] = phase[0]
+
+    column = lax.broadcasted_iota(jnp.int32, (1, depth), 1)
+    column_y = column // slot_rows
+    column_kind = lax.rem(column, slot_rows) // wide
+    column_d = lax.rem(column, wide) // nz
+    picks = [[(column_y == dy) & (column_d == d) for d in range(channels)] for dy in range(3)]
+    z_row = lax.broadcasted_iota(jnp.int32, (nz, depth), 0)
+    z_column = lax.rem(lax.broadcasted_iota(jnp.int32, (nz, depth), 1), nz)
+    bands = [z_column == lax.rem(z_row + dz - 1 + nz, nz) for dz in range(3)]
+    is_low = jnp.broadcast_to(column_kind, (nz, depth)) == 1
+    for dx in range(3):
+        for c in range(channels):
+            values = jnp.zeros((nz, depth), f32)
+            for dz in range(3):
+                line = jnp.zeros((1, depth), f32)
+                for dy in range(3):
+                    for d in range(channels):
+                        line = jnp.where(
+                            picks[dy][d], 0.5 * stencil[c, d, dy * 9 + dz * 3 + dx], line
+                        )
+                values = values + jnp.where(bands[dz], line, 0.0)
+            high = values.astype(bf16).astype(f32)
+            low = values - high
+            at = (dx * channels + c) * nz
+            matrix[at : at + nz, :] = jnp.where(is_low, low, high).astype(bf16)
+
+    for step in range(1, groups):
+        table_copy(step, turned(my_r, -step, groups)).wait_recv()
+    for source in range(groups):
+        heard = tables[source]
+        named = (heard[:, TARGET : TARGET + 1] == my_r.astype(f32)) & (
+            heard[:, LISTED : LISTED + 1] == 1.0
+        )
+        for rank in range(CAP):
+            chosen = named & (heard[:, RANK : RANK + 1] == float(rank))
+            line = jnp.sum(jnp.where(chosen, heard, 0.0), axis=0, keepdims=True)
+            missing = 1.0 - line[:, LISTED : LISTED + 1]
+            line = line + jnp.where(lane_ids[:1] == TANGENT, missing, 0.0)
+            at = source * CAP + rank
+            slots[at : at + 1, :] = line
+
+    def slot_value(load, index):
+        return jnp.broadcast_to(slots[pl.ds(load, 1), :][:, index : index + 1], (8, 128))
+
+    def force_copy(index, dy, dz):
+        y_at, z_at = block(dy, dz)
+        return pltpu.make_async_remote_copy(
+            src_ref=force_out.at[index], dst_ref=force.at[:, y_at, z_at],
+            send_sem=force_send.at[index], recv_sem=force_recv.at[index],
+            device_id=mate_id(*others[index]), device_id_type=MESH,
+        )
+
+    for index, (dy, dz) in enumerate(mates):
+        load = turned(my_y, dy, ngy) * ngz + turned(my_z, dz, ngz)
+        strain_of = [slot_value(load, j) for j in range(strains)]
+        for c in range(channels):
+            for y in range(y_here):
+                value = polar[0, c, 0, y] * strain_of[0]
+                for j in range(1, strains):
+                    value = value + polar[0, c, j, y] * strain_of[j]
+                if (dy, dz) == (0, 0):
+                    force[c, my_y * y_here + y, own_z, :] = value
+                else:
+                    force_out[index, c, y] = value
+        if (dy, dz) != (0, 0):
+            force_copy(index, 0, 0).start()
+
+    for index, (dy, dz) in enumerate(others):
+        phase_copy(index, -dy, -dz).wait_recv()
+    tangent_row = slots[pl.ds(my_load, 1), :][:, TANGENT : TANGENT + 1]
+    my_tangent = jnp.broadcast_to(tangent_row, (nz, nx))
+    inverse_tangent = 1.0 / my_tangent
+    for y in range(ny):
+        second = phase_all[y] == 1
+        mod = jnp.where(second, my_tangent, 1.0)
+        mod_mid[y] = mod
+        mod_low[y] = pltpu.roll(mod, nx - 1, 1)
+        mod_high[y] = pltpu.roll(mod, 1, 1)
+        mod_inv[y] = jnp.where(second, inverse_tangent, 1.0)
+    ones = jnp.ones((nz, nx), f32)
+    inverse_centre = [1.0 / (ones * stencil[c, c, 13]) for c in range(channels)]
+
+    def put(buffer, y, c, value):
+        both = jnp.concatenate([value, value * mod_mid[y]], axis=1)
+        high = both.astype(bf16)
+        low = (both - high.astype(f32)).astype(bf16)
+        at = pl.multiple_of((y + 1) * slot_rows + c * nz, 16)
+        spread[buffer, pl.ds(at, nz), :] = high
+        spread[buffer, pl.ds(at + wide, nz), :] = high
+        spread[buffer, pl.ds(at + 2 * wide, nz), :] = low
+
+    def wrap(buffer):
+        spread[buffer, 0:slot_rows, :] = spread[buffer, ny * slot_rows : (ny + 1) * slot_rows, :]
+        spread[buffer, (ny + 1) * slot_rows : (ny + 2) * slot_rows, :] = spread[
+            buffer, slot_rows : 2 * slot_rows, :
+        ]
+
+    for index, (dy, dz) in enumerate(others):
+        force_copy(index, -dy, -dz).wait_recv()
+    first_weight, weights = chebyshev_weights(SWEEPS)
+    for y in range(ny):
+        for c in range(channels):
+            value = first_weight * (force[c, y] * inverse_centre[c])
+            update[c, y] = value
+            field_now[c, y] = value
+            put(0, y, c, value)
+    wrap(0)
+
+    def sweep_row(buffer, y, old_weight, new_weight, last):
+        at = y * slot_rows if isinstance(y, int) else pl.multiple_of(y * slot_rows, 16)
+        product = jnp.dot(
+            matrix[...], spread[buffer, pl.ds(at, depth), :], preferred_element_type=f32
+        )
+        for c in range(channels):
+            parts = []
+            for dx, mod in enumerate((mod_low, mod_mid, mod_high)):
+                row = (dx * channels + c) * nz
+                parts.append(
+                    mod[y] * product[row : row + nz, :nx] + product[row : row + nz, nx:]
+                )
+            stiff = parts[1] + pltpu.roll(parts[0], 1, 1) + pltpu.roll(parts[2], nx - 1, 1)
+            residual = (force[c, y] - stiff * mod_inv[y]) * inverse_centre[c]
+            step = old_weight * update[c, y] + new_weight * residual
+            value = field_now[c, y] + step
+            field_now[c, y] = value
+            if not last:
+                update[c, y] = step
+                put(1 - buffer, y, c, value)
+
+    def sweep(k, carry):
+        old_weight, new_weight = jnp.float32(weights[0][0]), jnp.float32(weights[0][1])
+        for position in range(1, len(weights) - 1):
+            old_weight = jnp.where(k == position, weights[position][0], old_weight)
+            new_weight = jnp.where(k == position, weights[position][1], new_weight)
+        buffer = lax.rem(k, 2)
+        for y in range(ny):
+            sweep_row(buffer, y, old_weight, new_weight, False)
+        wrap(1 - buffer)
+        return carry
+
+    lax.fori_loop(0, len(weights) - 1, sweep, 0)
+
+    def field_copy(dy, dz, y, load):
+        to_y, to_z = turned(my_y, dy, ngy), turned(my_z, dz, ngz)
+        z_at = pl.ds(pl.multiple_of(to_z * z_here, 8), z_here)
+        return pltpu.make_async_remote_copy(
+            src_ref=field_now.at[:, to_y * y_here + y, z_at],
+            dst_ref=fields.at[0, load, :, y],
+            send_sem=field_send.at[dy, dz, y], recv_sem=field_recv.at[dy, dz, y],
+            device_id={"gy": to_y, "gz": to_z}, device_id_type=MESH,
+        )
+
+    final_buffer = (len(weights) - 1) % 2
+    for dy in list(range(1, ngy)) + [0]:
+        for y in range(y_here):
+            row = turned(my_y, dy, ngy) * y_here + y
+            sweep_row(final_buffer, row, weights[-1][0], weights[-1][1], True)
+            for dz in list(range(1, ngz)) + [0]:
+                if (dy, dz) != (0, 0):
+                    field_copy(dy, dz, y, my_load).start()
+                else:
+                    for c in range(channels):
+                        fields[0, my_load, c, y] = field_now[c, row, own_z, :]
+
+    seconds = [phase[0, y] == 1 for y in range(y_here)]
+    for dy, dz in mates:
+        load = turned(my_y, -dy, ngy) * ngz + turned(my_z, -dz, ngz)
+        if (dy, dz) != (0, 0):
+            for y in range(y_here):
+                field_copy(dy, dz, y, load).wait_recv()
+        slope = slot_value(load, TANGENT)
+        totals_of = [jnp.zeros((8, 128), f32) for _ in range(strains)]
+        for y in range(y_here):
+            mod = jnp.where(seconds[y], slope, 1.0)
+            for c in range(channels):
+                flux = mod * fields[0, load, c, y]
+                for j in range(strains):
+                    totals_of[j] = totals_of[j] + polar[0, c, j, y] * flux
+        for j in range(strains):
+            sums[j, pl.ds(load, 1), :] = jnp.sum(totals_of[j], axis=0, keepdims=True)
+    ones_here = jnp.zeros((8, 128), f32)
+    for y in range(y_here):
+        ones_here = ones_here + jnp.where(seconds[y], 1.0, 0.0)
+    second_count = jnp.sum(jnp.sum(ones_here, axis=0, keepdims=True), axis=1, keepdims=True)
+    slot_table = slots[...]
+    mod_sum = second_count * slot_table[:, TANGENT : TANGENT + 1] + (
+        float(y_here * z_here * nx) - second_count
+    )
+    share = jnp.where(lane_ids < strains, slot_table * mod_sum, 0.0)
+    for j in range(strains):
+        share = share + jnp.where(
+            lane_ids == j, jnp.sum(sums[j], axis=1, keepdims=True), 0.0
+        )
+    partials[len(others)] = share * (1.0 / (ny * nz * nx))
+
+    def part_copy(index):
+        return pltpu.make_async_remote_copy(
+            src_ref=partials.at[len(others)], dst_ref=partials.at[index],
+            send_sem=part_send.at[index], recv_sem=part_recv.at[index],
+            device_id=mate_id(*others[index]), device_id_type=MESH,
+        )
+
+    for index in range(len(others)):
+        part_copy(index).start()
+    for index in range(len(others)):
+        part_copy(index).wait_recv()
+    total = partials[0]
+    for index in range(1, len(mates)):
+        total = total + partials[index]
+    totals[my_r] = total
+
+    def total_copy(step, owner):
+        return pltpu.make_async_remote_copy(
+            src_ref=totals.at[my_r], dst_ref=totals.at[owner],
+            send_sem=total_send.at[step], recv_sem=total_recv.at[step],
+            device_id={"rve": turned(my_r, step, groups)}, device_id_type=MESH,
+        )
+
+    for step in range(1, groups):
+        total_copy(step, my_r).start()
+    for step in range(1, groups):
+        total_copy(step, turned(my_r, -step, groups)).wait_recv()
+    mine = tables[my_r]
+    answer = jnp.zeros((8, 128), f32)
+    for group in range(groups):
+        for rank in range(CAP):
+            chosen = (mine[:, TARGET : TARGET + 1] == float(group)) & (
+                mine[:, RANK : RANK + 1] == float(rank)
+            )
+            line = totals[group, pl.ds(my_r * CAP + rank, 1), :]
+            answer = answer + jnp.where(chosen, line, 0.0)
+    rows_out[...] = answer[:listed, :strains]
+
+    for step in range(1, groups):
+        table_copy(step, my_r).wait_send()
+        total_copy(step, my_r).wait_send()
+    for index, (dy, dz) in enumerate(others):
+        phase_copy(index, 0, 0).wait_send()
+        force_copy(index, 0, 0).wait_send()
+        part_copy(index).wait_send()
+        for y in range(y_here):
+            field_copy(dy, dz, y, my_load).wait_send()
+
+
+def fused_body(strain, tangent, yield_list, destination, phase_map, polarization, stencil):
+    groups, ngy, ngz = (lax.axis_size(name) for name in ("rve", "gy", "gz"))
+    channels = polarization.shape[1]
+    strains = polarization.shape[2]
+    y_here, z_here, nx = polarization.shape[3:]
+    ny, nz = y_here * ngy, z_here * ngz
+    loads = groups * CAP
+    count = ngy * ngz
+    f32 = jnp.float32
+    slot_rows = 3 * channels * nz
+    vmem = pl.BlockSpec(memory_space=pltpu.VMEM)
+    smem = pl.BlockSpec(memory_space=pltpu.SMEM)
+    cell = pltpu.VMEM((ny, nz, nx), f32)
+    vector = pltpu.VMEM((channels, ny, nz, nx), f32)
+
+    def dma(*shape):
+        return pltpu.SemaphoreType.DMA(shape)
+
+    return pl.pallas_call(
+        functools.partial(kernel, groups, ngy, ngz),
+        out_shape=(
+            jax.ShapeDtypeStruct((1, loads, channels, y_here, z_here, nx), f32),
+            jax.ShapeDtypeStruct((yield_list.shape[0], strains), f32),
+        ),
+        in_specs=[smem, smem, smem, smem, smem, vmem, vmem],
+        out_specs=(vmem, vmem),
+        scratch_shapes=[
+            pltpu.VMEM((groups, 8, 128), f32),
+            pltpu.VMEM((loads, 128), f32),
+            pltpu.VMEM((ny, nz, nx), jnp.int32),
+            pltpu.VMEM((count, channels, y_here, z_here, nx), f32),
+            vector,
+            pltpu.VMEM((3 * channels * nz, 3 * slot_rows), jnp.bfloat16),
+            pltpu.VMEM((2, (ny + 2) * slot_rows, 2 * nx), jnp.bfloat16),
+            vector,
+            vector,
+            cell, cell, cell, cell,
+            pltpu.VMEM((strains, loads, 128), f32),
+            pltpu.VMEM((count, 8, 128), f32),
+            pltpu.VMEM((groups, 8, 128), f32),
+            dma(groups), dma(groups), dma(count), dma(count), dma(count), dma(count),
+            dma(ngy, ngz, y_here), dma(ngy, ngz, y_here),
+            dma(count), dma(count), dma(groups), dma(groups),
+        ],
+        compiler_params=pltpu.CompilerParams(
+            collective_id=0, has_side_effects=True, vmem_limit_bytes=40 * 1024 * 1024
+        ),
+    )(strain, tangent, yield_list, destination, stencil, phase_map, polarization)
+
+
+def body_for(mesh):
+    def chosen(*arguments):
+        strain, _, yield_list, _, phase_map, _, _ = arguments
+        loads = lax.axis_size("rve") * CAP
+        one_load_each = lax.axis_size("gy") * lax.axis_size("gz") == loads
+        tiled = phase_map.shape[2] == 8 and phase_map.shape[3] == 128 and loads == 8
+        if one_load_each and tiled and yield_list.shape[0] <= 8:
+            return fused_body(*arguments)
+        return body(*arguments)
+
+    return chosen
+
+
 def solution(mesh):
     return jax.shard_map(
-        body,
+        body_for(mesh),
         mesh=mesh,
         in_specs=(
             P("rve", None),

time: 928 us -> 55 us (0.06); the launches traced: 914 us -> 54.7 us
  other arithmetic: 802 us -> 0 us
  Pallas kernels: 0 us -> 48.9 us
  waiting for transfers between devices: 39.9 us -> 0 us
  starting transfers between devices: 30.4 us -> 0 us
  local copies, waits for them, and re-layouts: 24.1 us -> 5.14 us
  blocking collectives: 12.4 us -> 0 us
    another operation x15 -> x0, other arithmetic: 793 us -> none  [apply_stiffness(): return jnp.stack(running, axis=1)]
    pallas_call x0 -> x1, Pallas kernels: none -> 48.9 us  [fused_body(): pl.pallas_call(functools.partial(kernel, groups, ngy, ngz), out_shape=(ja...]
    ppermute x24 -> x0, waiting for transfers between devices: 35.2 us -> none  [the longest x12 18.5 us: padded(): lax.ppermute(lax.slice_in_dim(block, 0, width, axis=dim), axis, backward)]
    slice x42 -> x0, local copies, waits for them, and re-layouts: 20 us -> none  [the longest x18 8.36 us: apply_stiffness(): rolled = jnp.roll(shifted, -shift_x, axis=4)]
    ppermute x24 -> x0, starting transfers between devices: 19 us -> none  [the longest x12 10.8 us: padded(): lax.ppermute(lax.slice_in_dim(block, 0, width, axis=dim), axis, backward)]
    psum x1 -> x0, blocking collectives: 12.4 us -> none  [body(): summed = lax.psum(partial_value, ('gy', 'gz')) / total_cells]
    all_to_all x2 -> x0, starting transfers between devices: 11.3 us -> none  [the longest x1 6.32 us: body(): lax.all_to_all(parcel, 'rve', split_axis=0, concat_axis=0, tiled=True)]
  transfers between devices with their start and end apart: 26 -> 0, of which waited for: 23 -> 0; matrix products, arithmetic and copies ran while one was open for 2% -> 0% of each run, Pallas kernels for 0% -> 0%
where the time goes in v1:
time: 55 us; the launch traced here: 54.7 us
  Pallas kernels  48.9 us (89%)
  local copies, waits for them, and re-layouts  5.14 us (9%)
  between operations  0.66 us (1%)
    pallas_call x1, Pallas kernels, fused_body(): pl.pallas_call(functools.partial(kernel, groups, ngy, ngz), out_shape=(ja...  48.9 us
    unnamed x15, local copies, waits for them, and re-layouts  5.14 us

profile of v1, /device:TPU:0, one launch (start us, length us, event | category | flops | bytes accessed | tf_op | source)
XLA Modules:
  0.0 54.7 jit_solution(13309842235174892651)
XLA Ops:
  0.6 0.0 copy-start.5
  0.6 0.0 copy-start.4
  0.7 0.8 %copy.9.destination = s32[4,1]{1,0:T(4,128)S(1)} copy(s32[4,1]{0,1:T(1,128)} %param.10) | data formatting | bytes 32 | tf_op args[3]
  1.4 0.0 copy-done.5
  1.4 0.0 copy-done.4
  1.4 0.0 copy-start
  1.4 1.0 %copy-done = f32[1,3,6,4,8,128]{5,4,3,2,1,0:T(8,128)S(1)} copy-done((f32[1,3,6,4,8,128]{5,4,3,2,1,0:T(8,128)S(1)}, f32[1,3,6,4,8,128]{5,4,3,2,1,0:T(8,128)}, u32[]{:S(2)}) %copy-start) | copy-done | bytes 294936
  2.4 0.0 copy-start.1
  2.4 0.7 %copy-done.1 = s32[1,4,8,128]{3,2,1,0:T(8,128)S(1)} copy-done((s32[1,4,8,128]{3,2,1,0:T(8,128)S(1)}, s32[1,4,8,128]{3,2,1,0:T(8,128)}, u32[]{:S(2)}) %copy-start.1) | copy-done | bytes 16408
  3.1 0.0 copy-start.2
  3.1 0.7 %copy-done.2 = f32[3,3,27]{2,1,0:T(4,128)S(1)} copy-done((f32[3,3,27]{2,1,0:T(4,128)S(1)}, f32[3,3,27]{2,1,0:T(4,128)}, u32[]{:S(2)}) %copy-start.2) | copy-done | bytes 996
  3.8 0.0 copy-start.3
  3.8 0.7 %copy-done.3 = f32[8,6]{1,0:T(8,128)S(1)} copy-done((f32[8,6]{1,0:T(8,128)S(1)}, f32[8,6]{1,0:T(8,128)}, u32[]{:S(2)}) %copy-start.3) | copy-done | bytes 216
  4.5 48.9 %shard_map.86 = (f32[1,8,3,4,8,128]{5,4,3,2,1,0:T(8,128)S(1)}, f32[4,6]{1,0:T(4,128)S(1)}) custom-call(f32[8,6]{1,0:T(8,128)S(1)} %copy-done.3, f32[8]{0:T(128)S(1)} %copy-done.4, s32[4]{0:T(128)S(1)} %copy-done.5, s32[4,1]{1,0:T(4,128)S(1)} %copy.9.destination, f32[3,3,27]{2,1,0:T(4,128)S(1)} %copy-done.2, s32[1,4,8,128]{3,2,1,0:T(8,128)S(1)} %copy-done.1, ...), custom_call_target="tpu_custom_call" | custom-call | tf_op jit(solution)/shard_map/pallas_call | solution.py:503
  53.4 0.7 %copy.12 = f32[1,8,3,4,8,128]{5,4,3,2,1,0:T(8,128)} copy(f32[1,8,3,4,8,128]{5,4,3,2,1,0:T(8,128)S(1)} %get-tuple-element.4) | data formatting | bytes 786432
  54.1 0.6 %copy.13 = f32[4,6]{1,0:T(4,128)} copy(f32[4,6]{1,0:T(4,128)S(1)} %get-tuple-element.5) | data formatting | bytes 192
Async XLA Ops:
  0.6 0.8 %copy-start.5 = (s32[4]{0:T(128)S(1)}, s32[4]{0:T(128)}, u32[]{:S(2)}) copy-start(s32[4]{0:T(128)} %yield_list.1) | copy-start | bytes 52
  0.6 0.8 %copy-start.4 = (f32[8]{0:T(128)S(1)}, f32[8]{0:T(128)}, u32[]{:S(2)}) copy-start(f32[8]{0:T(128)} %tangent.1) | copy-start | bytes 100
  1.4 1.0 %copy-start = (f32[1,3,6,4,8,128]{5,4,3,2,1,0:T(8,128)S(1)}, f32[1,3,6,4,8,128]{5,4,3,2,1,0:T(8,128)}, u32[]{:S(2)}) copy-start(f32[1,3,6,4,8,128]{5,4,3,2,1,0:T(8,128)} %polar.1) | copy-start | bytes 884740
  2.4 0.7 %copy-start.1 = (s32[1,4,8,128]{3,2,1,0:T(8,128)S(1)}, s32[1,4,8,128]{3,2,1,0:T(8,128)}, u32[]{:S(2)}) copy-start(s32[1,4,8,128]{3,2,1,0:T(8,128)} %phase.1) | copy-start | bytes 49156
  3.1 0.7 %copy-start.2 = (f32[3,3,27]{2,1,0:T(4,128)S(1)}, f32[3,3,27]{2,1,0:T(4,128)}, u32[]{:S(2)}) copy-start(f32[3,3,27]{2,1,0:T(4,128)} %stencil.1) | copy-start | bytes 2920
  3.8 0.7 %copy-start.3 = (f32[8,6]{1,0:T(8,128)S(1)}, f32[8,6]{1,0:T(8,128)}, u32[]{:S(2)}) copy-start(f32[8,6]{1,0:T(8,128)} %strain.1) | copy-start | bytes 580

commit v2 on v1

--- a/solution.py
+++ b/solution.py
@@ -239,6 +239,47 @@
     own_y, own_z = block(0, 0)
     phase_all[own_y, own_z, :] = phase[0]
 
+    for step in range(1, groups):
+        table_copy(step, turned(my_r, -step, groups)).wait_recv()
+    for source in range(groups):
+        heard = tables[source]
+        named = (heard[:, TARGET : TARGET + 1] == my_r.astype(f32)) & (
+            heard[:, LISTED : LISTED + 1] == 1.0
+        )
+        for rank in range(CAP):
+            chosen = named & (heard[:, RANK : RANK + 1] == float(rank))
+            line = jnp.sum(jnp.where(chosen, heard, 0.0), axis=0, keepdims=True)
+            missing = 1.0 - line[:, LISTED : LISTED + 1]
+            line = line + jnp.where(lane_ids[:1] == TANGENT, missing, 0.0)
+            at = source * CAP + rank
+            slots[at : at + 1, :] = line
+
+    def slot_value(load, index):
+        return jnp.broadcast_to(slots[pl.ds(load, 1), :][:, index : index + 1], (8, 128))
+
+    def force_copy(index, dy, dz):
+        y_at, z_at = block(dy, dz)
+        return pltpu.make_async_remote_copy(
+            src_ref=force_out.at[index], dst_ref=force.at[:, y_at, z_at],
+            send_sem=force_send.at[index], recv_sem=force_recv.at[index],
+            device_id=mate_id(*others[index]), device_id_type=MESH,
+        )
+
+    for index, (dy, dz) in enumerate(mates):
+        load = turned(my_y, dy, ngy) * ngz + turned(my_z, dz, ngz)
+        strain_of = [slot_value(load, j) for j in range(strains)]
+        for c in range(channels):
+            for y in range(y_here):
+                value = polar[0, c, 0, y] * strain_of[0]
+                for j in range(1, strains):
+                    value = value + polar[0, c, j, y] * strain_of[j]
+                if (dy, dz) == (0, 0):
+                    force[c, my_y * y_here + y, own_z, :] = value
+                else:
+                    force_out[index, c, y] = value
+        if (dy, dz) != (0, 0):
+            force_copy(index, 0, 0).start()
+
     column = lax.broadcasted_iota(jnp.int32, (1, depth), 1)
     column_y = column // slot_rows
     column_kind = lax.rem(column, slot_rows) // wide
@@ -263,47 +304,6 @@
             low = values - high
             at = (dx * channels + c) * nz
             matrix[at : at + nz, :] = jnp.where(is_low, low, high).astype(bf16)
-
-    for step in range(1, groups):
-        table_copy(step, turned(my_r, -step, groups)).wait_recv()
-    for source in range(groups):
-        heard = tables[source]
-        named = (heard[:, TARGET : TARGET + 1] == my_r.astype(f32)) & (
-            heard[:, LISTED : LISTED + 1] == 1.0
-        )
-        for rank in range(CAP):
-            chosen = named & (heard[:, RANK : RANK + 1] == float(rank))
-            line = jnp.sum(jnp.where(chosen, heard, 0.0), axis=0, keepdims=True)
-            missing = 1.0 - line[:, LISTED : LISTED + 1]
-            line = line + jnp.where(lane_ids[:1] == TANGENT, missing, 0.0)
-            at = source * CAP + rank
-            slots[at : at + 1, :] = line
-
-    def slot_value(load, index):
-        return jnp.broadcast_to(slots[pl.ds(load, 1), :][:, index : index + 1], (8, 128))
-
-    def force_copy(index, dy, dz):
-        y_at, z_at = block(dy, dz)
-        return pltpu.make_async_remote_copy(
-            src_ref=force_out.at[index], dst_ref=force.at[:, y_at, z_at],
-            send_sem=force_send.at[index], recv_sem=force_recv.at[index],
-            device_id=mate_id(*others[index]), device_id_type=MESH,
-        )
-
-    for index, (dy, dz) in enumerate(mates):
-        load = turned(my_y, dy, ngy) * ngz + turned(my_z, dz, ngz)
-        strain_of = [slot_value(load, j) for j in range(strains)]
-        for c in range(channels):
-            for y in range(y_here):
-                value = polar[0, c, 0, y] * strain_of[0]
-                for j in range(1, strains):
-                    value = value + polar[0, c, j, y] * strain_of[j]
-                if (dy, dz) == (0, 0):
-                    force[c, my_y * y_here + y, own_z, :] = value
-                else:
-                    force_out[index, c, y] = value
-        if (dy, dz) != (0, 0):
-            force_copy(index, 0, 0).start()
 
     for index, (dy, dz) in enumerate(others):
         phase_copy(index, -dy, -dz).wait_recv()

time: 55 us -> 55 us (level)
  no operation moved by 1% of the time
where the time goes in v2:
time: 55 us; the launch traced here: 54.7 us
  Pallas kernels  48.9 us (89%)
  local copies, waits for them, and re-layouts  5.14 us (9%)
  between operations  0.66 us (1%)
    pallas_call x1, Pallas kernels, fused_body(): pl.pallas_call(functools.partial(kernel, groups, ngy, ngz), out_shape=(ja...  48.9 us
    unnamed x15, local copies, waits for them, and re-layouts  5.14 us

profile of v2, /device:TPU:0, one launch (start us, length us, event | category | flops | bytes accessed | tf_op | source)
XLA Modules:
  0.0 54.7 jit_solution(15633173729846640495)
XLA Ops:
  0.6 0.0 copy-start.5
  0.6 0.0 copy-start.4
  0.7 0.8 %copy.9.destination = s32[4,1]{1,0:T(4,128)S(1)} copy(s32[4,1]{0,1:T(1,128)} %param.10) | data formatting | bytes 32 | tf_op args[3]
  1.4 0.0 copy-done.5
  1.4 0.0 copy-done.4
  1.4 0.0 copy-start
  1.4 1.0 %copy-done = f32[1,3,6,4,8,128]{5,4,3,2,1,0:T(8,128)S(1)} copy-done((f32[1,3,6,4,8,128]{5,4,3,2,1,0:T(8,128)S(1)}, f32[1,3,6,4,8,128]{5,4,3,2,1,0:T(8,128)}, u32[]{:S(2)}) %copy-start) | copy-done | bytes 294936
  2.4 0.0 copy-start.1
  2.4 0.7 %copy-done.1 = s32[1,4,8,128]{3,2,1,0:T(8,128)S(1)} copy-done((s32[1,4,8,128]{3,2,1,0:T(8,128)S(1)}, s32[1,4,8,128]{3,2,1,0:T(8,128)}, u32[]{:S(2)}) %copy-start.1) | copy-done | bytes 16408
  3.1 0.0 copy-start.2
  3.1 0.7 %copy-done.2 = f32[3,3,27]{2,1,0:T(4,128)S(1)} copy-done((f32[3,3,27]{2,1,0:T(4,128)S(1)}, f32[3,3,27]{2,1,0:T(4,128)}, u32[]{:S(2)}) %copy-start.2) | copy-done | bytes 996
  3.8 0.0 copy-start.3
  3.8 0.7 %copy-done.3 = f32[8,6]{1,0:T(8,128)S(1)} copy-done((f32[8,6]{1,0:T(8,128)S(1)}, f32[8,6]{1,0:T(8,128)}, u32[]{:S(2)}) %copy-start.3) | copy-done | bytes 216
  4.5 48.9 %shard_map.86 = (f32[1,8,3,4,8,128]{5,4,3,2,1,0:T(8,128)S(1)}, f32[4,6]{1,0:T(4,128)S(1)}) custom-call(f32[8,6]{1,0:T(8,128)S(1)} %copy-done.3, f32[8]{0:T(128)S(1)} %copy-done.4, s32[4]{0:T(128)S(1)} %copy-done.5, s32[4,1]{1,0:T(4,128)S(1)} %copy.9.destination, f32[3,3,27]{2,1,0:T(4,128)S(1)} %copy-done.2, s32[1,4,8,128]{3,2,1,0:T(8,128)S(1)} %copy-done.1, ...), custom_call_target="tpu_custom_call" | custom-call | tf_op jit(solution)/shard_map/pallas_call | solution.py:503
  53.4 0.7 %copy.12 = f32[1,8,3,4,8,128]{5,4,3,2,1,0:T(8,128)} copy(f32[1,8,3,4,8,128]{5,4,3,2,1,0:T(8,128)S(1)} %get-tuple-element.4) | data formatting | bytes 786432
  54.1 0.6 %copy.13 = f32[4,6]{1,0:T(4,128)} copy(f32[4,6]{1,0:T(4,128)S(1)} %get-tuple-element.5) | data formatting | bytes 192
Async XLA Ops:
  0.6 0.8 %copy-start.5 = (s32[4]{0:T(128)S(1)}, s32[4]{0:T(128)}, u32[]{:S(2)}) copy-start(s32[4]{0:T(128)} %yield_list.1) | copy-start | bytes 52
  0.6 0.8 %copy-start.4 = (f32[8]{0:T(128)S(1)}, f32[8]{0:T(128)}, u32[]{:S(2)}) copy-start(f32[8]{0:T(128)} %tangent.1) | copy-start | bytes 100
  1.4 1.0 %copy-start = (f32[1,3,6,4,8,128]{5,4,3,2,1,0:T(8,128)S(1)}, f32[1,3,6,4,8,128]{5,4,3,2,1,0:T(8,128)}, u32[]{:S(2)}) copy-start(f32[1,3,6,4,8,128]{5,4,3,2,1,0:T(8,128)} %polar.1) | copy-start | bytes 884740
  2.4 0.7 %copy-start.1 = (s32[1,4,8,128]{3,2,1,0:T(8,128)S(1)}, s32[1,4,8,128]{3,2,1,0:T(8,128)}, u32[]{:S(2)}) copy-start(s32[1,4,8,128]{3,2,1,0:T(8,128)} %phase.1) | copy-start | bytes 49156
  3.1 0.7 %copy-start.2 = (f32[3,3,27]{2,1,0:T(4,128)S(1)}, f32[3,3,27]{2,1,0:T(4,128)}, u32[]{:S(2)}) copy-start(f32[3,3,27]{2,1,0:T(4,128)} %stencil.1) | copy-start | bytes 2920
  3.8 0.7 %copy-start.3 = (f32[8,6]{1,0:T(8,128)S(1)}, f32[8,6]{1,0:T(8,128)}, u32[]{:S(2)}) copy-start(f32[8,6]{1,0:T(8,128)} %strain.1) | copy-start | bytes 580

commit v3 on v2

--- a/solution.py
+++ b/solution.py
@@ -367,18 +367,20 @@
                 update[c, y] = step
                 put(1 - buffer, y, c, value)
 
-    def sweep(k, carry):
-        old_weight, new_weight = jnp.float32(weights[0][0]), jnp.float32(weights[0][1])
-        for position in range(1, len(weights) - 1):
-            old_weight = jnp.where(k == position, weights[position][0], old_weight)
-            new_weight = jnp.where(k == position, weights[position][1], new_weight)
-        buffer = lax.rem(k, 2)
-        for y in range(ny):
-            sweep_row(buffer, y, old_weight, new_weight, False)
-        wrap(1 - buffer)
+    def sweep_pair(pair, carry):
+        for buffer in range(2):
+            k = pair * 2 + buffer
+            old_weight, new_weight = jnp.float32(weights[0][0]), jnp.float32(weights[0][1])
+            for position in range(1, len(weights) - 1):
+                old_weight = jnp.where(k == position, weights[position][0], old_weight)
+                new_weight = jnp.where(k == position, weights[position][1], new_weight)
+            for y in range(ny):
+                sweep_row(buffer, y, old_weight, new_weight, False)
+            wrap(1 - buffer)
         return carry
 
-    lax.fori_loop(0, len(weights) - 1, sweep, 0)
+    assert len(weights) % 2 == 1
+    lax.fori_loop(0, (len(weights) - 1) // 2, sweep_pair, 0)
 
     def field_copy(dy, dz, y, load):
         to_y, to_z = turned(my_y, dy, ngy), turned(my_z, dz, ngz)

time: 55 us -> 43.9 us (0.80)
  Pallas kernels: 48.9 us -> 37.7 us
    pallas_call x1, Pallas kernels: 48.9 us -> 37.7 us  [fused_body(): pl.pallas_call(functools.partial(kernel, groups, ngy, ngz), out_shape=(ja...]
where the time goes in v3:
time: 43.9 us; the launch traced here: 43.5 us
  Pallas kernels  37.7 us (86%)
  local copies, waits for them, and re-layouts  5.14 us (12%)
  between operations  0.66 us (2%)
    pallas_call x1, Pallas kernels, fused_body(): pl.pallas_call(functools.partial(kernel, groups, ngy, ngz), out_shape=(ja...  37.7 us
    unnamed x15, local copies, waits for them, and re-layouts  5.14 us

profile of v3, /device:TPU:0, one launch (start us, length us, event | category | flops | bytes accessed | tf_op | source)
XLA Modules:
  0.0 43.5 jit_solution(6005219442441997744)
XLA Ops:
  0.6 0.0 copy-start.5
  0.6 0.0 copy-start.4
  0.7 0.8 %copy.9.destination = s32[4,1]{1,0:T(4,128)S(1)} copy(s32[4,1]{0,1:T(1,128)} %param.10) | data formatting | bytes 32 | tf_op args[3]
  1.4 0.0 copy-done.5
  1.4 0.0 copy-done.4
  1.4 0.0 copy-start
  1.4 1.0 %copy-done = f32[1,3,6,4,8,128]{5,4,3,2,1,0:T(8,128)S(1)} copy-done((f32[1,3,6,4,8,128]{5,4,3,2,1,0:T(8,128)S(1)}, f32[1,3,6,4,8,128]{5,4,3,2,1,0:T(8,128)}, u32[]{:S(2)}) %copy-start) | copy-done | bytes 294936
  2.4 0.0 copy-start.1
  2.4 0.7 %copy-done.1 = s32[1,4,8,128]{3,2,1,0:T(8,128)S(1)} copy-done((s32[1,4,8,128]{3,2,1,0:T(8,128)S(1)}, s32[1,4,8,128]{3,2,1,0:T(8,128)}, u32[]{:S(2)}) %copy-start.1) | copy-done | bytes 16408
  3.1 0.0 copy-start.2
  3.1 0.7 %copy-done.2 = f32[3,3,27]{2,1,0:T(4,128)S(1)} copy-done((f32[3,3,27]{2,1,0:T(4,128)S(1)}, f32[3,3,27]{2,1,0:T(4,128)}, u32[]{:S(2)}) %copy-start.2) | copy-done | bytes 996
  3.8 0.0 copy-start.3
  3.8 0.7 %copy-done.3 = f32[8,6]{1,0:T(8,128)S(1)} copy-done((f32[8,6]{1,0:T(8,128)S(1)}, f32[8,6]{1,0:T(8,128)}, u32[]{:S(2)}) %copy-start.3) | copy-done | bytes 216
  4.5 37.7 %shard_map.86 = (f32[1,8,3,4,8,128]{5,4,3,2,1,0:T(8,128)S(1)}, f32[4,6]{1,0:T(4,128)S(1)}) custom-call(f32[8,6]{1,0:T(8,128)S(1)} %copy-done.3, f32[8]{0:T(128)S(1)} %copy-done.4, s32[4]{0:T(128)S(1)} %copy-done.5, s32[4,1]{1,0:T(4,128)S(1)} %copy.9.destination, f32[3,3,27]{2,1,0:T(4,128)S(1)} %copy-done.2, s32[1,4,8,128]{3,2,1,0:T(8,128)S(1)} %copy-done.1, ...), custom_call_target="tpu_custom_call" | custom-call | tf_op jit(solution)/shard_map/pallas_call | solution.py:505
  42.2 0.7 %copy.12 = f32[1,8,3,4,8,128]{5,4,3,2,1,0:T(8,128)} copy(f32[1,8,3,4,8,128]{5,4,3,2,1,0:T(8,128)S(1)} %get-tuple-element.4) | data formatting | bytes 786432
  43.0 0.6 %copy.13 = f32[4,6]{1,0:T(4,128)} copy(f32[4,6]{1,0:T(4,128)S(1)} %get-tuple-element.5) | data formatting | bytes 192
Async XLA Ops:
  0.6 0.8 %copy-start.5 = (s32[4]{0:T(128)S(1)}, s32[4]{0:T(128)}, u32[]{:S(2)}) copy-start(s32[4]{0:T(128)} %yield_list.1) | copy-start | bytes 52
  0.6 0.8 %copy-start.4 = (f32[8]{0:T(128)S(1)}, f32[8]{0:T(128)}, u32[]{:S(2)}) copy-start(f32[8]{0:T(128)} %tangent.1) | copy-start | bytes 100
  1.4 1.0 %copy-start = (f32[1,3,6,4,8,128]{5,4,3,2,1,0:T(8,128)S(1)}, f32[1,3,6,4,8,128]{5,4,3,2,1,0:T(8,128)}, u32[]{:S(2)}) copy-start(f32[1,3,6,4,8,128]{5,4,3,2,1,0:T(8,128)} %polar.1) | copy-start | bytes 884740
  2.4 0.7 %copy-start.1 = (s32[1,4,8,128]{3,2,1,0:T(8,128)S(1)}, s32[1,4,8,128]{3,2,1,0:T(8,128)}, u32[]{:S(2)}) copy-start(s32[1,4,8,128]{3,2,1,0:T(8,128)} %phase.1) | copy-start | bytes 49156
  3.1 0.7 %copy-start.2 = (f32[3,3,27]{2,1,0:T(4,128)S(1)}, f32[3,3,27]{2,1,0:T(4,128)}, u32[]{:S(2)}) copy-start(f32[3,3,27]{2,1,0:T(4,128)} %stencil.1) | copy-start | bytes 2920
  3.8 0.7 %copy-start.3 = (f32[8,6]{1,0:T(8,128)S(1)}, f32[8,6]{1,0:T(8,128)}, u32[]{:S(2)}) copy-start(f32[8,6]{1,0:T(8,128)} %strain.1) | copy-start | bytes 580

commit v4 on v3

--- a/solution.py
+++ b/solution.py
@@ -346,11 +346,13 @@
             put(0, y, c, value)
     wrap(0)
 
-    def sweep_row(buffer, y, old_weight, new_weight, last):
+    def row_product(buffer, y):
         at = y * slot_rows if isinstance(y, int) else pl.multiple_of(y * slot_rows, 16)
-        product = jnp.dot(
+        return jnp.dot(
             matrix[...], spread[buffer, pl.ds(at, depth), :], preferred_element_type=f32
         )
+
+    def finish_row(product, buffer, y, old_weight, new_weight, last):
         for c in range(channels):
             parts = []
             for dx, mod in enumerate((mod_low, mod_mid, mod_high)):
@@ -375,7 +377,7 @@
                 old_weight = jnp.where(k == position, weights[position][0], old_weight)
                 new_weight = jnp.where(k == position, weights[position][1], new_weight)
             for y in range(ny):
-                sweep_row(buffer, y, old_weight, new_weight, False)
+                finish_row(row_product(buffer, y), buffer, y, old_weight, new_weight, False)
             wrap(1 - buffer)
         return carry
 
@@ -393,16 +395,24 @@
         )
 
     final_buffer = (len(weights) - 1) % 2
-    for dy in list(range(1, ngy)) + [0]:
-        for y in range(y_here):
-            row = turned(my_y, dy, ngy) * y_here + y
-            sweep_row(final_buffer, row, weights[-1][0], weights[-1][1], True)
-            for dz in list(range(1, ngz)) + [0]:
-                if (dy, dz) != (0, 0):
-                    field_copy(dy, dz, y, my_load).start()
-                else:
-                    for c in range(channels):
-                        fields[0, my_load, c, y] = field_now[c, row, own_z, :]
+    last_rows = [
+        (dy, y, turned(my_y, dy, ngy) * y_here + y)
+        for dy in list(range(1, ngy)) + [0]
+        for y in range(y_here)
+    ]
+    product = row_product(final_buffer, last_rows[0][2])
+    for place, (dy, y, row) in enumerate(last_rows):
+        later = None
+        if place + 1 < len(last_rows):
+            later = row_product(final_buffer, last_rows[place + 1][2])
+        finish_row(product, final_buffer, row, weights[-1][0], weights[-1][1], True)
+        product = later
+        for dz in list(range(1, ngz)) + [0]:
+            if (dy, dz) != (0, 0):
+                field_copy(dy, dz, y, my_load).start()
+            else:
+                for c in range(channels):
+                    fields[0, my_load, c, y] = field_now[c, row, own_z, :]
 
     seconds = [phase[0, y] == 1 for y in range(y_here)]
     for dy, dz in mates:

time: 43.9 us -> 43.5 us (level)
  no operation moved by 1% of the time
where the time goes in v4:
time: 43.5 us; the launch traced here: 43.1 us
  Pallas kernels  37.3 us (86%)
  local copies, waits for them, and re-layouts  5.14 us (12%)
  between operations  0.66 us (2%)
    pallas_call x1, Pallas kernels, fused_body(): pl.pallas_call(functools.partial(kernel, groups, ngy, ngz), out_shape=(ja...  37.3 us
    unnamed x15, local copies, waits for them, and re-layouts  5.14 us

profile of v4, /device:TPU:0, one launch (start us, length us, event | category | flops | bytes accessed | tf_op | source)
XLA Modules:
  0.0 43.1 jit_solution(9583451671457160257)
XLA Ops:
  0.6 0.0 copy-start.5
  0.6 0.0 copy-start.4
  0.7 0.8 %copy.9.destination = s32[4,1]{1,0:T(4,128)S(1)} copy(s32[4,1]{0,1:T(1,128)} %param.10) | data formatting | bytes 32 | tf_op args[3]
  1.4 0.0 copy-done.5
  1.4 0.0 copy-done.4
  1.4 0.0 copy-start
  1.4 1.0 %copy-done = f32[1,3,6,4,8,128]{5,4,3,2,1,0:T(8,128)S(1)} copy-done((f32[1,3,6,4,8,128]{5,4,3,2,1,0:T(8,128)S(1)}, f32[1,3,6,4,8,128]{5,4,3,2,1,0:T(8,128)}, u32[]{:S(2)}) %copy-start) | copy-done | bytes 294936
  2.4 0.0 copy-start.1
  2.4 0.7 %copy-done.1 = s32[1,4,8,128]{3,2,1,0:T(8,128)S(1)} copy-done((s32[1,4,8,128]{3,2,1,0:T(8,128)S(1)}, s32[1,4,8,128]{3,2,1,0:T(8,128)}, u32[]{:S(2)}) %copy-start.1) | copy-done | bytes 16408
  3.1 0.0 copy-start.2
  3.1 0.7 %copy-done.2 = f32[3,3,27]{2,1,0:T(4,128)S(1)} copy-done((f32[3,3,27]{2,1,0:T(4,128)S(1)}, f32[3,3,27]{2,1,0:T(4,128)}, u32[]{:S(2)}) %copy-start.2) | copy-done | bytes 996
  3.8 0.0 copy-start.3
  3.8 0.7 %copy-done.3 = f32[8,6]{1,0:T(8,128)S(1)} copy-done((f32[8,6]{1,0:T(8,128)S(1)}, f32[8,6]{1,0:T(8,128)}, u32[]{:S(2)}) %copy-start.3) | copy-done | bytes 216
  4.5 37.3 %shard_map.86 = (f32[1,8,3,4,8,128]{5,4,3,2,1,0:T(8,128)S(1)}, f32[4,6]{1,0:T(4,128)S(1)}) custom-call(f32[8,6]{1,0:T(8,128)S(1)} %copy-done.3, f32[8]{0:T(128)S(1)} %copy-done.4, s32[4]{0:T(128)S(1)} %copy-done.5, s32[4,1]{1,0:T(4,128)S(1)} %copy.9.destination, f32[3,3,27]{2,1,0:T(4,128)S(1)} %copy-done.2, s32[1,4,8,128]{3,2,1,0:T(8,128)S(1)} %copy-done.1, ...), custom_call_target="tpu_custom_call" | custom-call | tf_op jit(solution)/shard_map/pallas_call | solution.py:515
  41.8 0.7 %copy.12 = f32[1,8,3,4,8,128]{5,4,3,2,1,0:T(8,128)} copy(f32[1,8,3,4,8,128]{5,4,3,2,1,0:T(8,128)S(1)} %get-tuple-element.4) | data formatting | bytes 786432
  42.5 0.6 %copy.13 = f32[4,6]{1,0:T(4,128)} copy(f32[4,6]{1,0:T(4,128)S(1)} %get-tuple-element.5) | data formatting | bytes 192
Async XLA Ops:
  0.6 0.8 %copy-start.5 = (s32[4]{0:T(128)S(1)}, s32[4]{0:T(128)}, u32[]{:S(2)}) copy-start(s32[4]{0:T(128)} %yield_list.1) | copy-start | bytes 52
  0.6 0.8 %copy-start.4 = (f32[8]{0:T(128)S(1)}, f32[8]{0:T(128)}, u32[]{:S(2)}) copy-start(f32[8]{0:T(128)} %tangent.1) | copy-start | bytes 100
  1.4 1.0 %copy-start = (f32[1,3,6,4,8,128]{5,4,3,2,1,0:T(8,128)S(1)}, f32[1,3,6,4,8,128]{5,4,3,2,1,0:T(8,128)}, u32[]{:S(2)}) copy-start(f32[1,3,6,4,8,128]{5,4,3,2,1,0:T(8,128)} %polar.1) | copy-start | bytes 884740
  2.4 0.7 %copy-start.1 = (s32[1,4,8,128]{3,2,1,0:T(8,128)S(1)}, s32[1,4,8,128]{3,2,1,0:T(8,128)}, u32[]{:S(2)}) copy-start(s32[1,4,8,128]{3,2,1,0:T(8,128)} %phase.1) | copy-start | bytes 49156
  3.1 0.7 %copy-start.2 = (f32[3,3,27]{2,1,0:T(4,128)S(1)}, f32[3,3,27]{2,1,0:T(4,128)}, u32[]{:S(2)}) copy-start(f32[3,3,27]{2,1,0:T(4,128)} %stencil.1) | copy-start | bytes 2920
  3.8 0.7 %copy-start.3 = (f32[8,6]{1,0:T(8,128)S(1)}, f32[8,6]{1,0:T(8,128)}, u32[]{:S(2)}) copy-start(f32[8,6]{1,0:T(8,128)} %strain.1) | copy-start | bytes 580

commit v5 on v4

--- a/solution.py
+++ b/solution.py
@@ -376,8 +376,11 @@
             for position in range(1, len(weights) - 1):
                 old_weight = jnp.where(k == position, weights[position][0], old_weight)
                 new_weight = jnp.where(k == position, weights[position][1], new_weight)
+            product = row_product(buffer, 0)
             for y in range(ny):
-                finish_row(row_product(buffer, y), buffer, y, old_weight, new_weight, False)
+                later = row_product(buffer, y + 1) if y + 1 < ny else None
+                finish_row(product, buffer, y, old_weight, new_weight, False)
+                product = later
             wrap(1 - buffer)
         return carry
 

time: 43.5 us -> 43.4 us (level)
  no operation moved by 1% of the time
where the time goes in v5:
time: 43.4 us; the launch traced here: 43.1 us
  Pallas kernels  37.3 us (86%)
  local copies, waits for them, and re-layouts  5.14 us (12%)
  between operations  0.66 us (2%)
    pallas_call x1, Pallas kernels, fused_body(): pl.pallas_call(functools.partial(kernel, groups, ngy, ngz), out_shape=(ja...  37.3 us
    unnamed x15, local copies, waits for them, and re-layouts  5.14 us

profile of v5, /device:TPU:0, one launch (start us, length us, event | category | flops | bytes accessed | tf_op | source)
XLA Modules:
  0.0 43.1 jit_solution(7892663482441387892)
XLA Ops:
  0.6 0.0 copy-start.5
  0.6 0.0 copy-start.4
  0.7 0.8 %copy.9.destination = s32[4,1]{1,0:T(4,128)S(1)} copy(s32[4,1]{0,1:T(1,128)} %param.10) | data formatting | bytes 32 | tf_op args[3]
  1.4 0.0 copy-done.5
  1.4 0.0 copy-done.4
  1.4 0.0 copy-start
  1.4 1.0 %copy-done = f32[1,3,6,4,8,128]{5,4,3,2,1,0:T(8,128)S(1)} copy-done((f32[1,3,6,4,8,128]{5,4,3,2,1,0:T(8,128)S(1)}, f32[1,3,6,4,8,128]{5,4,3,2,1,0:T(8,128)}, u32[]{:S(2)}) %copy-start) | copy-done | bytes 294936
  2.4 0.0 copy-start.1
  2.4 0.7 %copy-done.1 = s32[1,4,8,128]{3,2,1,0:T(8,128)S(1)} copy-done((s32[1,4,8,128]{3,2,1,0:T(8,128)S(1)}, s32[1,4,8,128]{3,2,1,0:T(8,128)}, u32[]{:S(2)}) %copy-start.1) | copy-done | bytes 16408
  3.1 0.0 copy-start.2
  3.1 0.7 %copy-done.2 = f32[3,3,27]{2,1,0:T(4,128)S(1)} copy-done((f32[3,3,27]{2,1,0:T(4,128)S(1)}, f32[3,3,27]{2,1,0:T(4,128)}, u32[]{:S(2)}) %copy-start.2) | copy-done | bytes 996
  3.8 0.0 copy-start.3
  3.8 0.7 %copy-done.3 = f32[8,6]{1,0:T(8,128)S(1)} copy-done((f32[8,6]{1,0:T(8,128)S(1)}, f32[8,6]{1,0:T(8,128)}, u32[]{:S(2)}) %copy-start.3) | copy-done | bytes 216
  4.5 37.3 %shard_map.86 = (f32[1,8,3,4,8,128]{5,4,3,2,1,0:T(8,128)S(1)}, f32[4,6]{1,0:T(4,128)S(1)}) custom-call(f32[8,6]{1,0:T(8,128)S(1)} %copy-done.3, f32[8]{0:T(128)S(1)} %copy-done.4, s32[4]{0:T(128)S(1)} %copy-done.5, s32[4,1]{1,0:T(4,128)S(1)} %copy.9.destination, f32[3,3,27]{2,1,0:T(4,128)S(1)} %copy-done.2, s32[1,4,8,128]{3,2,1,0:T(8,128)S(1)} %copy-done.1, ...), custom_call_target="tpu_custom_call" | custom-call | tf_op jit(solution)/shard_map/pallas_call | solution.py:518
  41.8 0.7 %copy.12 = f32[1,8,3,4,8,128]{5,4,3,2,1,0:T(8,128)} copy(f32[1,8,3,4,8,128]{5,4,3,2,1,0:T(8,128)S(1)} %get-tuple-element.4) | data formatting | bytes 786432
  42.5 0.6 %copy.13 = f32[4,6]{1,0:T(4,128)} copy(f32[4,6]{1,0:T(4,128)S(1)} %get-tuple-element.5) | data formatting | bytes 192
Async XLA Ops:
  0.6 0.8 %copy-start.5 = (s32[4]{0:T(128)S(1)}, s32[4]{0:T(128)}, u32[]{:S(2)}) copy-start(s32[4]{0:T(128)} %yield_list.1) | copy-start | bytes 52
  0.6 0.8 %copy-start.4 = (f32[8]{0:T(128)S(1)}, f32[8]{0:T(128)}, u32[]{:S(2)}) copy-start(f32[8]{0:T(128)} %tangent.1) | copy-start | bytes 100
  1.4 1.0 %copy-start = (f32[1,3,6,4,8,128]{5,4,3,2,1,0:T(8,128)S(1)}, f32[1,3,6,4,8,128]{5,4,3,2,1,0:T(8,128)}, u32[]{:S(2)}) copy-start(f32[1,3,6,4,8,128]{5,4,3,2,1,0:T(8,128)} %polar.1) | copy-start | bytes 884740
  2.4 0.7 %copy-start.1 = (s32[1,4,8,128]{3,2,1,0:T(8,128)S(1)}, s32[1,4,8,128]{3,2,1,0:T(8,128)}, u32[]{:S(2)}) copy-start(s32[1,4,8,128]{3,2,1,0:T(8,128)} %phase.1) | copy-start | bytes 49156
  3.1 0.7 %copy-start.2 = (f32[3,3,27]{2,1,0:T(4,128)S(1)}, f32[3,3,27]{2,1,0:T(4,128)}, u32[]{:S(2)}) copy-start(f32[3,3,27]{2,1,0:T(4,128)} %stencil.1) | copy-start | bytes 2920
  3.8 0.7 %copy-start.3 = (f32[8,6]{1,0:T(8,128)S(1)}, f32[8,6]{1,0:T(8,128)}, u32[]{:S(2)}) copy-start(f32[8,6]{1,0:T(8,128)} %strain.1) | copy-start | bytes 580
